TPU v7x, 32 devices: a whole 2x2x4 slice. The times are simulated.
32 devices in a mesh: groups: 2 (over y), segment: 8 (over z, x), template: 2 (over core).
Axes of the slice: x: 2, y: 2, z: 4, core: 2. Of those that a mesh axis runs over, the one named last changes fastest.
Arguments:
- strain_frames: bfloat16 [64, 16384], P('segment'), may hold values from -6 to 6
- frame_slot: int32 [8, 8], replicated, may hold values from 0 to 7, as said below
- templates: bfloat16 [4, 2, 131072], P(('groups', 'template'), None, 'segment'), parts along dimension 0, may hold values from -6 to 6
- bin_edges: int32 [4, 3], P(('groups', 'template')), parts along dimension 0, may hold values from 16384 to 114687, as said below
Outputs:
- snr_series: bfloat16 [8, 4, 131072], P('segment', ('groups', 'template')), parts along dimension 1
- chisq_series: bfloat16 [8, 4, 131072], P('segment', ('groups', 'template')), parts along dimension 1
- peak_newsnr: float32 [8, 4], P('segment', ('groups', 'template')), parts along dimension 1
There are 2 independent parts, one for each index of `groups`. A program takes and returns all parts, laid end to end along the dimension named above; an argument that names none is the same for every part. Nothing has to cross between parts.
Inputs may be any that keep to these rules, and one draw needn't show every extreme that they name: Each column frame_slot[:, j] is a permutation of 0 to 7. `bin_edges`: edge number e of a template lies in [(2 e + 1) * 16384, (2 e + 3) * 16384), so the edges rise.
All inputs are finite; a program needn't handle non-finite values.
Results may differ from a plain program's by a relative error of at most 0.011.
Values may be sent and summed in bfloat16 or wider, within the bound.
A program may use at most 64 MiB of HBM per device.

v0:
```python
import math
import jax
import jax.numpy as jnp
from jax import lax
from jax.sharding import PartitionSpec as P

RADIX_A = 64
RADIX_B = 32
RADIX_C = 128


def dft_table(length, orient):
    counter = jnp.arange(length, dtype=jnp.int32)
    product = counter[:, None] * counter[None, :] % length
    angles = orient * 2.0 * math.pi / length * product.astype(jnp.float32)
    cosine = jnp.cos(angles)
    sine = jnp.sin(angles)
    upper = jnp.stack([cosine, -sine], axis=1)
    lower = jnp.stack([sine, cosine], axis=1)
    return jnp.stack([upper, lower], axis=0).astype(jnp.bfloat16)


def rotate(values, phase_index, modulus, orient):
    angles = orient * 2.0 * math.pi / modulus * (phase_index % modulus).astype(jnp.float32)
    cosine = jnp.cos(angles)
    sine = jnp.sin(angles)
    real_part = values[0] * cosine - values[1] * sine
    imag_part = values[0] * sine + values[1] * cosine
    return jnp.stack([real_part, imag_part]).astype(jnp.bfloat16)


def later_passes(level_one, orient, table_three):
    length = RADIX_A * RADIX_B * RADIX_C
    inner = RADIX_B * RADIX_C
    grid_one = (
        jnp.arange(RADIX_A, dtype=jnp.int32)[:, None] * jnp.arange(inner, dtype=jnp.int32)[None, :]
    )
    turned = rotate(level_one, grid_one, length, orient).reshape(2, RADIX_A, RADIX_B, RADIX_C)
    level_two = jnp.einsum(
        "cjdp,dkpr->ckjr", dft_table(RADIX_B, orient), turned, preferred_element_type=jnp.float32
    )
    grid_two = (
        jnp.arange(RADIX_B, dtype=jnp.int32)[:, None]
        * jnp.arange(RADIX_C, dtype=jnp.int32)[None, :]
    )
    turned_two = rotate(level_two, grid_two, inner, orient)
    level_three = jnp.einsum(
        "cldr,dkjr->ckjl", table_three, turned_two, preferred_element_type=jnp.float32
    )
    rows = table_three.shape[1]
    return jnp.transpose(level_three, (0, 3, 2, 1)).reshape(2, rows * inner * RADIX_A // RADIX_C)


def forward_spectrum(real_signal):
    inner = RADIX_B * RADIX_C
    start = real_signal.reshape(RADIX_A, inner)
    table_one = dft_table(RADIX_A, -1.0)[:, :, 0, :]
    level_one = jnp.einsum("ckp,pq->ckq", table_one, start, preferred_element_type=jnp.float32)
    table_three = dft_table(RADIX_C, -1.0)[:, : RADIX_C // 2]
    return later_passes(level_one, -1.0, table_three)


def inverse_kept(masked):
    inner = RADIX_B * RADIX_C
    start = masked.reshape(2, RADIX_A // 2, inner)
    table_one = dft_table(RADIX_A, 1.0)[:, :, :, : RADIX_A // 2]
    level_one = jnp.einsum("ckdp,dpq->ckq", table_one, start, preferred_element_type=jnp.float32)
    table_three = dft_table(RADIX_C, 1.0)[:, RADIX_C // 4 : RADIX_C // 4 + RADIX_C // 2]
    return later_passes(level_one, 1.0, table_three)


def filter_template(spectrum, template, edges):
    length = RADIX_A * RADIX_B * RADIX_C
    kept = length // 2
    temp_real = template[0].astype(jnp.float32)
    temp_imag = template[1].astype(jnp.float32)
    corr_real = spectrum[0] * temp_real + spectrum[1] * temp_imag
    corr_imag = spectrum[1] * temp_real - spectrum[0] * temp_imag
    power = temp_real * temp_real + temp_imag * temp_imag
    total = jnp.sum(power)
    bin_index = jnp.arange(kept, dtype=jnp.int32)
    label = (
        (bin_index >= edges[0]).astype(jnp.int32)
        + (bin_index >= edges[1]).astype(jnp.int32)
        + (bin_index >= edges[2]).astype(jnp.int32)
    )
    pieces = []
    shares = []
    for number in range(4):
        inside = (label == number).astype(jnp.float32)
        shares.append(jnp.sum(power * inside) / total)
        masked = jnp.stack([corr_real * inside, corr_imag * inside]).astype(jnp.bfloat16)
        pieces.append(inverse_kept(masked) / length)
    summed = pieces[0] + pieces[1] + pieces[2] + pieces[3]
    scale = length / total
    snr = jnp.sqrt((summed[0] * summed[0] + summed[1] * summed[1]) * scale)
    chisq = jnp.zeros_like(snr)
    for number in range(4):
        diff_real = pieces[number][0] - shares[number] * summed[0]
        diff_imag = pieces[number][1] - shares[number] * summed[1]
        chisq = chisq + diff_real * diff_real + diff_imag * diff_imag
    chisq = chisq * scale
    reduced = chisq / 6.0
    weighted = snr * ((1.0 + reduced * reduced * reduced) / 2.0) ** (-1.0 / 6.0)
    newsnr = jnp.where(reduced > 1.0, weighted, snr)
    return (snr.astype(jnp.bfloat16), chisq.astype(jnp.bfloat16), jnp.max(newsnr))


def local(strain_frames, frame_slot, templates, bin_edges):
    segments_count = lax.axis_size("segment")
    position = lax.axis_index("segment")
    frame_length = strain_frames.shape[1]
    length = RADIX_A * RADIX_B * RADIX_C
    kept = length // 2
    counter = jnp.arange(segments_count, dtype=jnp.int32)
    slot_now = lax.dynamic_slice_in_dim(frame_slot, position, 1, 1)[:, 0]
    next_index = jnp.minimum(position + 1, segments_count - 1)
    slot_next = lax.dynamic_slice_in_dim(frame_slot, next_index, 1, 1)[:, 0]

    def arrange(slots, frames):
        selector = (counter[:, None] == slots[None, :]).astype(jnp.bfloat16)
        return (
            jnp.dot(selector, frames, preferred_element_type=jnp.float32)
            .astype(jnp.bfloat16)
            .reshape(kept)
        )

    following_rows = jnp.concatenate(
        [strain_frames[1:], jnp.zeros((1, frame_length), jnp.bfloat16)], axis=0
    )
    outgoing = jnp.stack([strain_frames, following_rows], axis=1)
    received = lax.all_to_all(outgoing, "segment", split_axis=0, concat_axis=0, tiled=True)
    leading = arrange(slot_now, received[:, 0])
    trailing = arrange(slot_next, received[:, 1])
    segment_data = jnp.concatenate([leading, trailing])
    whole_templates = lax.all_gather(templates, "segment", axis=2, tiled=True)
    spectrum = forward_spectrum(segment_data)
    snr_one, chisq_one, peak_one = filter_template(spectrum, whole_templates[0], bin_edges[0])
    snr_rows = [snr_one]
    chisq_rows = [chisq_one]
    peak_rows = [peak_one]
    snr_series = jnp.stack(snr_rows)[None]
    chisq_series = jnp.stack(chisq_rows)[None]
    peak_newsnr = jnp.stack(peak_rows)[None]
    return (snr_series, chisq_series, peak_newsnr)


def solution(mesh):
    in_specs = (
        P("segment", None),
        P(),
        P(("groups", "template"), None, "segment"),
        P(("groups", "template"), None),
    )
    out_specs = (
        P("segment", ("groups", "template"), None),
        P("segment", ("groups", "template"), None),
        P("segment", ("groups", "template")),
    )
    return jax.shard_map(local, mesh=mesh, in_specs=in_specs, out_specs=out_specs, check_vma=False)
```

profile of v0, /device:TPU:0, one launch (start us, length us, event | category | flops | bytes accessed | tf_op | source)
XLA Modules:
  0.0 121.7 jit_solution(296445114597201190)
XLA Ops:
  0.6 1.0 slice.196
  1.7 1.0 pad_maximum_fusion
  2.7 1.3 %copy.65 = bf16[8,2,16384]{2,1,0:T(2,128)(2,1)} copy(bf16[8,2,16384]{2,0,1:T(8,128)(2,1)S(1)} %pad_maximum_fusion) | data formatting | bytes 1048576 | tf_op jit(solution)/shard_map/stack | solution.py:131
  4.1 7.3 %all-to-all-start = ((bf16[8,2,16384]{2,1,0:T(2,128)(2,1)}), bf16[8,2,16384]{2,1,0:T(2,128)(2,1)S(1)}, u32[]{:S(2)}, u32[]{:S(2)}) async-start(bf16[8,2,16384]{2,1,0:T(2,128)(2,1)} %copy.65), calls=%async_computation | async-start | bytes 1048576 | tf_op jit(solution)/shard_map/all_to_all | solution.py:132
  13.8 0.6 fusion.140
  14.4 35.5 %all_gather.3 = bf16[1,2,131072]{2,1,0:T(2,128)(2,1)S(1)} all-gather(bf16[1,2,16384]{2,1,0:T(2,128)(2,1)S(1)} %copy-done.3), channel_id=1, replica_groups=mesh['groups'=2,'segment'=8,'template'=2] {'segment'}, dimensions={2}, use_global_device_ids=true | all-gather | bytes 589824 | tf_op jit(solution)/shard_map/all_gather | solution.py:136
  49.9 4.1 %fusion.81 = (f32[131072]{0:T(1024)S(1)}, f32[131072]{0:T(1024)S(1)}, f32[]{:T(128)}, f32[1,1,131072]{2,1,0:T(1,128)S(1)}) fusion(bf16[1,2,131072]{2,1,0:T(2,128)(2,1)S(1)} %all_gather.3), kind=kLoop, calls=%fused_computation.186 | loop fusion | flops 786431 | bytes 2097156 | tf_op jit(solution)/shard_map/convert_element_type | solution.py:75
  54.0 2.9 %select_reduce_fusion.3 = (f32[]{:T(128)}, f32[]{:T(128)}, f32[]{:T(128)}, f32[]{:T(128)}) fusion(f32[131072]{0:T(1024)S(1)} %bitcast.310, s32[]{:T(128)} %bitcast.4, s32[]{:T(128)} %bitcast.3, s32[]{:T(128)} %bitcast.2), kind=kLoop, calls=%fused_computation.155 | loop fusion | flops 2621436 | bytes 524316 | tf_op jit(solution)/shard_map/reduce_sum | solution.py:91
  56.9 0.9 reshape.1209
  63.7 0.9 reshape.1210
  65.3 0.9 fusion.139
  67.9 4.8 %fusion.79 = (bf16[8,8,32,128]{3,1,2,0:T(8,128)(2,1)S(1)}, bf16[8,8,32,128]{3,1,2,0:T(8,128)(2,1)S(1)}) fusion(f32[2,64,4096]{2,1,0:T(8,128)S(1)} %fusion.57), kind=kLoop, calls=%fused_computation.184 | loop fusion | flops 5767168 | bytes 3145728
  72.9 0.5 convolution_bitcast_fusion.9
  74.3 1.1 copy.71
  75.8 1.1 copy.70
  77.3 3.3 %select_convert_fusion.5 = (bf16[1,32,4096]{2,1,0:T(8,128)(2,1)S(1)}, bf16[1,32,4096]{2,1,0:T(8,128)(2,1)S(1)}, bf16[1,32,4096]{2,1,0:T(8,128)(2,1)S(1)}, bf16[1,32,4096]{2,1,0:T(8,128)(2,1)S(1)}) fusion(s32[]{:T(128)} %bitcast.4, s32[]{:T(128)} %bitcast.3, s32[]{:T(128)} %bitcast.2, f32[1,32,4096]{2,1,0:T(8,128)S(1)} %squeeze.55, ...), kind=kLoop, calls=%fused_computation.170 | loop fusion | flops 2752512 | bytes 3145740 | tf_op jit(solution)/shard_map/convert.25
  80.5 2.3 %select_convert_fusion.6 = (bf16[1,32,4096]{2,1,0:T(8,128)(2,1)S(1)}, bf16[1,32,4096]{2,1,0:T(8,128)(2,1)S(1)}, bf16[1,32,4096]{2,1,0:T(8,128)(2,1)S(1)}, bf16[1...) fusion(bf16[1,32,4096]{2,1,0:T(8,128)(2,1)S(1)} %get-tuple-element.42, ...), kind=kLoop, calls=%fused_computation.171 | loop fusion | flops 2490368 | bytes 2097164 | tf_op jit(solution)/shard_map/convert.50
  83.3 4.6 %fusion.49 = (bf16[8,8,32,128]{3,1,2,0:T(8,128)(2,1)S(1)}, bf16[8,8,32,128]{3,1,2,0:T(8,128)(2,1)S(1)}) fusion(f32[2,64,4096]{2,1,0:T(8,128)S(1)} %convolution_bitcast_fusion.3), kind=kLoop, calls=%fused_computation.114 | loop fusion | flops 5767168 | bytes 3145728
  88.6 4.6 %fusion.51 = (bf16[8,8,32,128]{3,1,2,0:T(8,128)(2,1)S(1)}, bf16[8,8,32,128]{3,1,2,0:T(8,128)(2,1)S(1)}) fusion(f32[2,64,4096]{2,1,0:T(8,128)S(1)} %convolution_bitcast_fusion.2), kind=kLoop, calls=%fused_computation.116 | loop fusion | flops 5767168 | bytes 3145728
  94.0 4.6 %fusion.53 = (bf16[8,8,32,128]{3,1,2,0:T(8,128)(2,1)S(1)}, bf16[8,8,32,128]{3,1,2,0:T(8,128)(2,1)S(1)}) fusion(f32[2,64,4096]{2,1,0:T(8,128)S(1)} %convolution_bitcast_fusion.1), kind=kLoop, calls=%fused_computation.118 | loop fusion | flops 5767168 | bytes 3145728
  99.3 4.8 %fusion.55 = (bf16[8,8,32,128]{3,1,2,0:T(8,128)(2,1)S(1)}, bf16[8,8,32,128]{3,1,2,0:T(8,128)(2,1)S(1)}) fusion(f32[2,64,4096]{2,1,0:T(8,128)S(1)} %convolution_bitcast_fusion), kind=kLoop, calls=%fused_computation.120 | loop fusion | flops 5767168 | bytes 3145728
  106.3 1.3 %subtract_convert_fusion.4 = (bf16[1,64,32,128]{3,2,0,1:T(8,128)(2,1)S(1)}, bf16[1,64,32,128]{3,2,0,1:T(8,128)(2,1)S(1)}, bf16[1,64,32,128]{3,2,0,1:T(8,128)(2,1...) fusion(f32[2,64,32,128]{3,2,0,1:T(8,128)S(1)} %convolution_bitc, ...), kind=kLoop, calls=%fused_computation.90 | loop fusion | flops 8388608 | bytes 12615680 | tf_op jit(solution)/shard_map/convert.19
  109.0 0.5 add_add_fusion
  109.5 2.4 %broadcast_multiply_fusion = (f32[1,64,32,64]{1,2,0,3:T(8,128)S(1)}, bf16[1,64,32,64]{1,2,0,3:T(8,128)(2,1)}, bf16[1,64,32,64]{1,2,0,3:T(8,128)(2,1)}, f32[1,64,32,64]{1,2,0,3:T(8,128)S(1)}) fusion(f32[]{:T(128)S(6)} %div.55, f32[2,64,32,64]{1,2,0,3:T(8,128)S(1)} %get-tuple-element.79, f32[]{:T(128)S(6)} %div.59, f32[2,64,32,64]{1,2,0,3:T(8,128)S(1)} %fusion.1, ...), kind=kLoop, calls=%fused_computation.151 | loop fusion | flops 5111808 | bytes 6815764 | tf_op jit(solution)/shard_map/div | solution.py:103
  112.0 1.1 copy.86
  113.1 1.0 reshape.1304
  114.0 2.1 %copy.85 = bf16[1,64,32,64]{3,2,1,0:T(8,128)(2,1)S(1)} copy(bf16[1,64,32,64]{1,2,0,3:T(8,128)(2,1)} %get-tuple-element.12) | data formatting | bytes 524288 | tf_op jit(solution)/shard_map/convert_element_type | solution.py:106
  116.2 1.1 reshape.1302
  117.3 1.1 copy.84
  118.3 1.1 sqrt.17
  119.4 1.1 copy.87
  120.7 1.0 fusion.48
  (82 shorter events, 13.0 us)
Async XLA Ops:
  1.6 12.1 %copy-start.5 = (s32[1,3]{1,0:T(1,128)S(1)}, s32[1,3]{1,0:T(1,128)}, u32[]{:S(2)}) copy-start(s32[1,3]{1,0:T(1,128)} %param.7) | copy-start | bytes 40
  1.7 12.7 %copy-start.3 = (bf16[1,2,16384]{2,1,0:T(2,128)(2,1)S(1)}, bf16[1,2,16384]{2,1,0:T(2,128)(2,1)}, u32[]{:S(2)}) copy-start(bf16[1,2,16384]{2,1,0:T(2,128)(2,1)} %param.6) | copy-start | bytes 196612
  4.1 61.2 %all-to-all-start = ((bf16[8,2,16384]{2,1,0:T(2,128)(2,1)}), bf16[8,2,16384]{2,1,0:T(2,128)(2,1)S(1)}, u32[]{:S(2)}, u32[]{:S(2)}) async-start(bf16[8,2,16384]{2,1,0:T(2,128)(2,1)} %copy.65), calls=%async_computation | async-start | bytes 1048576 | tf_op jit(solution)/shard_map/all_to_all | solution.py:132
  49.9 14.7 %copy-start.4 = (s32[8,8]{1,0:T(8,128)S(1)}, s32[8,8]{1,0:T(8,128)}, u32[]{:S(2)}) copy-start(s32[8,8]{1,0:T(8,128)} %param.5) | copy-start | bytes 772
  75.8 1.5 %copy-start = (f32[1,32,4096]{2,1,0:T(8,128)S(1)}, f32[1,32,4096]{2,1,0:T(8,128)}, u32[]{:S(2)}) copy-start(f32[1,32,4096]{2,1,0:T(8,128)} %reshape.1209) | copy-start | bytes 1572868
  113.0 4.2 %copy-start.1 = (bf16[1,64,32,64]{1,2,0,3:T(8,128)(2,1)S(1)}, bf16[1,64,32,64]{1,2,0,3:T(8,128)(2,1)}, u32[]{:S(2)}) copy-start(bf16[1,64,32,64]{1,2,0,3:T(8,128)(2,1)} %get-tuple-element.31) | copy-start | bytes 786436
  119.4 1.3 %copy-start.2 = (f32[131072]{0:T(1024)S(1)}, f32[131072]{0:T(1024)}, u32[]{:S(2)}) copy-start(f32[131072]{0:T(1024)} %reshape.1304) | copy-start | bytes 1572868
where the time goes:
time: 122 us
  other arithmetic  44.6 us (37%)
  blocking collectives  35.5 us (29%)
  local copies, waits for them, and re-layouts  19.4 us (16%)
  matrix products  7.79 us (6%)
  starting transfers between devices  7.25 us (6%)
  between operations  7.15 us (6%)
    all_gather x1, blocking collectives, local(): whole_templates = lax.all_gather(templates, 'segment', axis=2, tiled=True)  35.5 us
    unnamed x5, other arithmetic  23.3 us
    another operation x19, other arithmetic  9.6 us
    all_to_all x1, starting transfers between devices, local(): lax.all_to_all(outgoing, 'segment', split_axis=0, concat_axis=0, tiled=True)  7.25 us
    convert_element_type x1, other arithmetic, filter_template(): temp_real = template[0].astype(jnp.float32)  4.07 us
    convert_element_type x2, local copies, waits for them, and re-layouts, filter_template(): chisq.astype(jnp.bfloat16)  3.2 us
    reduce_sum x1, other arithmetic, filter_template(): shares.append(jnp.sum(power * inside) / total)  2.89 us
  transfers between devices with their start and end apart: 1, of which 0 were waited for; matrix products, arithmetic and copies ran while one was open for 10% of the time, Pallas kernels for 0%

commit v1 on v0

--- a/solution.py
+++ b/solution.py
@@ -7,6 +7,18 @@
 RADIX_A = 64
 RADIX_B = 32
 RADIX_C = 128
+
+
+def gather_by_bits(shard, axis, dim):
+    ways, here = (lax.axis_size(axis), lax.axis_index(axis))
+    grown, reach = (shard, 1)
+    while reach < ways:
+        theirs = lax.ppermute(grown, axis, [(d, d ^ reach) for d in range(ways)])
+        mine_first = jnp.concatenate([grown, theirs], axis=dim)
+        theirs_first = jnp.concatenate([theirs, grown], axis=dim)
+        grown = jnp.where(here & reach == 0, mine_first, theirs_first)
+        reach = 2 * reach
+    return grown
 
 
 def dft_table(length, orient):
@@ -133,7 +145,7 @@
     leading = arrange(slot_now, received[:, 0])
     trailing = arrange(slot_next, received[:, 1])
     segment_data = jnp.concatenate([leading, trailing])
-    whole_templates = lax.all_gather(templates, "segment", axis=2, tiled=True)
+    whole_templates = gather_by_bits(templates, "segment", 2)
     spectrum = forward_spectrum(segment_data)
     snr_one, chisq_one, peak_one = filter_template(spectrum, whole_templates[0], bin_edges[0])
     snr_rows = [snr_one]

time: 122 us -> 111 us (0.910)
  blocking collectives: 35.5 us -> 0 us
  waiting for transfers between devices: 0.01 us -> 16.8 us
  starting transfers between devices: 7.25 us -> 13 us
  other arithmetic: 44.6 us -> 46.4 us
    all_gather x1 -> x0, blocking collectives: 35.5 us -> none  [local(): whole_templates = lax.all_gather(templates, 'segment', axis=2, tiled=True)]
    ppermute x0 -> x3, waiting for transfers between devices: none -> 16.8 us  [gather_by_bits(): theirs = lax.ppermute(grown, axis, [(d, d ^ reach) for d in range(ways)])]
    ppermute x0 -> x3, starting transfers between devices: none -> 8.08 us  [gather_by_bits(): theirs = lax.ppermute(grown, axis, [(d, d ^ reach) for d in range(ways)])]
    all_to_all x1, starting transfers between devices: 7.25 us -> 4.88 us  [local(): lax.all_to_all(outgoing, 'segment', split_axis=0, concat_axis=0, tiled=True)]
    select_n x0 -> x4, other arithmetic: none -> 1.64 us  [gather_by_bits(): grown = jnp.where(here & reach == 0, mine_first, theirs_first)]
  transfers between devices with their start and end apart: 1 -> 4, of which waited for: 0 -> 2; matrix products, arithmetic and copies ran while one was open for 10% -> 16% of each run, Pallas kernels for 0% -> 0%
where the time goes in v1:
time: 111 us
  other arithmetic  46.4 us (42%)
  local copies, waits for them, and re-layouts  19.5 us (18%)
  waiting for transfers between devices  16.8 us (15%)
  starting transfers between devices  13 us (12%)
  matrix products  7.97 us (7%)
  between operations  7.28 us (7%)
    unnamed x5, other arithmetic  23.1 us
    ppermute x3, waiting for transfers between devices, gather_by_bits(): theirs = lax.ppermute(grown, axis, [(d, d ^ reach) for d in range(ways)])  16.8 us
    another operation x19, other arithmetic  9.54 us
    ppermute x3, starting transfers between devices, gather_by_bits(): theirs = lax.ppermute(grown, axis, [(d, d ^ reach) for d in range(ways)])  8.08 us
    all_to_all x1, starting transfers between devices, local(): lax.all_to_all(outgoing, 'segment', split_axis=0, concat_axis=0, tiled=True)  4.88 us
    convert_element_type x1, other arithmetic, filter_template(): temp_real = template[0].astype(jnp.float32)  4.08 us
    convert_element_type x2, local copies, waits for them, and re-layouts, filter_template(): chisq.astype(jnp.bfloat16)  3.2 us
    reduce_sum x1, other arithmetic, filter_template(): shares.append(jnp.sum(power * inside) / total)  2.91 us
  transfers between devices with their start and end apart: 4, of which 2 were waited for; matrix products, arithmetic and copies ran while one was open for 16% of the time, Pallas kernels for 0%

profile of v1, /device:TPU:0, one launch (start us, length us, event | category | flops | bytes accessed | tf_op | source)
XLA Modules:
  0.0 110.9 jit_solution(11055131157901920321)
XLA Ops:
  0.6 3.0 %collective-permute-start = (bf16[1,2,16384]{2,1,0:T(2,128)(2,1)}, bf16[1,2,16384]{2,1,0:T(2,128)(2,1)S(1)}, u32[]{:S(2)}, u32[]{:S(2)}) collective-permute-start(bf16[1,2,16384]{2,1,0:T(2,128)(2,1)} %param.6), channel_id=1, source_target_pairs={{0,2},{2,0},{4,6},{6,4},{8,10},{10,8},{12,14},{14,12},{1,3},{3,1},... | collective-permute-start | bytes 196616 | tf_op jit(solution)/shard_map/ppermute | solution.py:16
  3.6 1.0 slice.196
  4.7 1.0 pad_maximum_fusion
  5.8 1.3 %copy.65 = bf16[8,2,16384]{2,1,0:T(2,128)(2,1)} copy(bf16[8,2,16384]{2,0,1:T(8,128)(2,1)S(1)} %pad_maximum_fusion) | data formatting | bytes 1048576 | tf_op jit(solution)/shard_map/stack | solution.py:143
  7.1 4.9 %all-to-all-start = ((bf16[8,2,16384]{2,1,0:T(2,128)(2,1)}), bf16[8,2,16384]{2,1,0:T(2,128)(2,1)S(1)}, u32[]{:S(2)}, u32[]{:S(2)}) async-start(bf16[8,2,16384]{2,1,0:T(2,128)(2,1)} %copy.65), calls=%async_computation | async-start | bytes 1048576 | tf_op jit(solution)/shard_map/all_to_all | solution.py:144
  16.0 2.1 %collective-permute-start.1 = (bf16[1,2,32768]{2,1,0:T(2,128)(2,1)S(1)}, bf16[1,2,32768]{2,1,0:T(2,128)(2,1)S(1)}, u32[]{:S(2)}, u32[]{:S(2)}) collective-permute-start(bf16[1,2,32768]{2,1,0:T(2,128)(2,1)S(1)} %broadcast_select_fusion.3), channel_id=1, source_target_pairs={{0,4},{2,6},{4,0},{6,2},{8,12},{10,14},{12,8},{14,10},{1,5},{3,7},... | collective-permute-start | bytes 393224 | tf_op jit(solution)/shard_map/ppermute | solution.py:16
  18.3 6.5 %collective-permute-done.1 = bf16[1,2,32768]{2,1,0:T(2,128)(2,1)S(1)} collective-permute-done((bf16[1,2,32768]{2,1,0:T(2,128)(2,1)S(1)}, bf16[1,2,32768]{2,1,0:T(2,128)(2,1)S(1)}, u32[]{:S(2)}, u32[]{:S(2)}) %collective-permute-start.1) | collective-permute-done | bytes 131104 | tf_op jit(solution)/shard_map/ppermute | solution.py:16
  25.2 3.0 %collective-permute-start.2 = (bf16[1,2,65536]{2,1,0:T(2,128)(2,1)S(1)}, bf16[1,2,65536]{2,1,0:T(2,128)(2,1)S(1)}, u32[]{:S(2)}, u32[]{:S(2)}) collective-permute-start(bf16[1,2,65536]{2,1,0:T(2,128)(2,1)S(1)} %broadcast_select_fusion.1), channel_id=1, source_target_pairs={{0,8},{2,10},{4,12},{6,14},{8,0},{10,2},{12,4},{14,6},{1,9},{3,11}... | collective-permute-start | bytes 786440 | tf_op jit(solution)/shard_map/ppermute | solution.py:16
  28.6 10.4 %collective-permute-done.2 = bf16[1,2,65536]{2,1,0:T(2,128)(2,1)S(1)} collective-permute-done((bf16[1,2,65536]{2,1,0:T(2,128)(2,1)S(1)}, bf16[1,2,65536]{2,1,0:T(2,128)(2,1)S(1)}, u32[]{:S(2)}, u32[]{:S(2)}) %collective-permute-start.2) | collective-permute-done | bytes 262176 | tf_op jit(solution)/shard_map/ppermute | solution.py:16
  39.8 4.1 %fusion.81 = (f32[131072]{0:T(1024)S(1)}, f32[131072]{0:T(1024)S(1)}, f32[]{:T(128)}, f32[1,1,131072]{2,1,0:T(1,128)S(1)}) fusion(bf16[1,2,131072]{2,1,0:T(2,128)(2,1)S(1)} %broadcast_select_fusion), kind=kLoop, calls=%fused_computation.189 | loop fusion | flops 786431 | bytes 2097156 | tf_op jit(solution)/shard_map/convert_element_type | solution.py:87
  43.8 0.9 reshape.1495
  45.4 2.9 %select_reduce_fusion.3 = (f32[]{:T(128)}, f32[]{:T(128)}, f32[]{:T(128)}, f32[]{:T(128)}) fusion(f32[131072]{0:T(1024)S(1)} %bitcast.316, s32[]{:T(128)} %bitcast.4, s32[]{:T(128)} %bitcast.3, s32[]{:T(128)} %bitcast.2), kind=kLoop, calls=%fused_computation.156 | loop fusion | flops 2621436 | bytes 524316 | tf_op jit(solution)/shard_map/reduce_sum | solution.py:103
  54.6 0.9 fusion.140
  57.3 4.6 %fusion.79 = (bf16[8,8,32,128]{3,1,2,0:T(8,128)(2,1)S(1)}, bf16[8,8,32,128]{3,1,2,0:T(8,128)(2,1)S(1)}) fusion(f32[2,64,4096]{2,1,0:T(8,128)S(1)} %fusion.57), kind=kLoop, calls=%fused_computation.185 | loop fusion | flops 5767168 | bytes 3145728
  63.6 1.1 copy.71
  65.1 1.1 copy.70
  66.5 3.2 %select_convert_fusion.5 = (bf16[1,32,4096]{2,1,0:T(8,128)(2,1)S(1)}, bf16[1,32,4096]{2,1,0:T(8,128)(2,1)S(1)}, bf16[1,32,4096]{2,1,0:T(8,128)(2,1)S(1)}, bf16[1,32,4096]{2,1,0:T(8,128)(2,1)S(1)}) fusion(s32[]{:T(128)} %bitcast.4, s32[]{:T(128)} %bitcast.3, s32[]{:T(128)} %bitcast.2, f32[1,32,4096]{2,1,0:T(8,128)S(1)} %squeeze.55, ...), kind=kLoop, calls=%fused_computation.171 | loop fusion | flops 2752512 | bytes 3145740 | tf_op jit(solution)/shard_map/convert.25
  69.7 2.3 %select_convert_fusion.6 = (bf16[1,32,4096]{2,1,0:T(8,128)(2,1)S(1)}, bf16[1,32,4096]{2,1,0:T(8,128)(2,1)S(1)}, bf16[1,32,4096]{2,1,0:T(8,128)(2,1)S(1)}, bf16[1...) fusion(bf16[1,32,4096]{2,1,0:T(8,128)(2,1)S(1)} %get-tuple-element.42, ...), kind=kLoop, calls=%fused_computation.172 | loop fusion | flops 2490368 | bytes 2097164 | tf_op jit(solution)/shard_map/convert.50
  72.5 4.6 %fusion.49 = (bf16[8,8,32,128]{3,1,2,0:T(8,128)(2,1)S(1)}, bf16[8,8,32,128]{3,1,2,0:T(8,128)(2,1)S(1)}) fusion(f32[2,64,4096]{2,1,0:T(8,128)S(1)} %convolution_bitcast_fusion.3), kind=kLoop, calls=%fused_computation.115 | loop fusion | flops 5767168 | bytes 3145728
  77.8 4.6 %fusion.51 = (bf16[8,8,32,128]{3,1,2,0:T(8,128)(2,1)S(1)}, bf16[8,8,32,128]{3,1,2,0:T(8,128)(2,1)S(1)}) fusion(f32[2,64,4096]{2,1,0:T(8,128)S(1)} %convolution_bitcast_fusion.2), kind=kLoop, calls=%fused_computation.117 | loop fusion | flops 5767168 | bytes 3145728
  83.2 4.6 %fusion.53 = (bf16[8,8,32,128]{3,1,2,0:T(8,128)(2,1)S(1)}, bf16[8,8,32,128]{3,1,2,0:T(8,128)(2,1)S(1)}) fusion(f32[2,64,4096]{2,1,0:T(8,128)S(1)} %convolution_bitcast_fusion.1), kind=kLoop, calls=%fused_computation.119 | loop fusion | flops 5767168 | bytes 3145728
  88.5 4.8 %fusion.55 = (bf16[8,8,32,128]{3,1,2,0:T(8,128)(2,1)S(1)}, bf16[8,8,32,128]{3,1,2,0:T(8,128)(2,1)S(1)}) fusion(f32[2,64,4096]{2,1,0:T(8,128)S(1)} %convolution_bitcast_fusion), kind=kLoop, calls=%fused_computation.121 | loop fusion | flops 5767168 | bytes 3145728
  95.5 1.3 %subtract_convert_fusion.4 = (bf16[1,64,32,128]{3,2,0,1:T(8,128)(2,1)S(1)}, bf16[1,64,32,128]{3,2,0,1:T(8,128)(2,1)S(1)}, bf16[1,64,32,128]{3,2,0,1:T(8,128)(2,1...) fusion(f32[2,64,32,128]{3,2,0,1:T(8,128)S(1)} %convolution_bitc, ...), kind=kLoop, calls=%fused_computation.90 | loop fusion | flops 8388608 | bytes 12615680 | tf_op jit(solution)/shard_map/convert.19
  98.7 2.4 %broadcast_multiply_fusion = (f32[1,64,32,64]{1,2,0,3:T(8,128)S(1)}, bf16[1,64,32,64]{1,2,0,3:T(8,128)(2,1)}, bf16[1,64,32,64]{1,2,0,3:T(8,128)(2,1)}, f32[1,64,32,64]{1,2,0,3:T(8,128)S(1)}) fusion(f32[]{:T(128)S(6)} %div.55, f32[2,64,32,64]{1,2,0,3:T(8,128)S(1)} %get-tuple-element.79, f32[]{:T(128)S(6)} %div.59, f32[2,64,32,64]{1,2,0,3:T(8,128)S(1)} %fusion.1, ...), kind=kLoop, calls=%fused_computation.152 | loop fusion | flops 5111808 | bytes 6815764 | tf_op jit(solution)/shard_map/div | solution.py:115
  101.2 1.1 copy.86
  102.3 1.0 reshape.1590
  103.3 2.1 %copy.85 = bf16[1,64,32,64]{3,2,1,0:T(8,128)(2,1)S(1)} copy(bf16[1,64,32,64]{1,2,0,3:T(8,128)(2,1)} %get-tuple-element.12) | data formatting | bytes 524288 | tf_op jit(solution)/shard_map/convert_element_type | solution.py:118
  105.4 1.1 reshape.1588
  106.5 1.1 copy.84
  107.6 1.1 sqrt.17
  108.6 1.1 copy.87
  109.9 1.0 fusion.48
  (92 shorter events, 17.7 us)
Async XLA Ops:
  0.6 15.2 %collective-permute-start = (bf16[1,2,16384]{2,1,0:T(2,128)(2,1)}, bf16[1,2,16384]{2,1,0:T(2,128)(2,1)S(1)}, u32[]{:S(2)}, u32[]{:S(2)}) collective-permute-start(bf16[1,2,16384]{2,1,0:T(2,128)(2,1)} %param.6), channel_id=1, source_target_pairs={{0,2},{2,0},{4,6},{6,4},{8,10},{10,8},{12,14},{14,12},{1,3},{3,1},... | collective-permute-start | bytes 196616 | tf_op jit(solution)/shard_map/ppermute | solution.py:16
  4.7 10.1 %copy-start.4 = (s32[8,8]{1,0:T(8,128)S(1)}, s32[8,8]{1,0:T(8,128)}, u32[]{:S(2)}) copy-start(s32[8,8]{1,0:T(8,128)} %param.5) | copy-start | bytes 772
  4.7 10.5 %copy-start.5 = (s32[1,3]{1,0:T(1,128)S(1)}, s32[1,3]{1,0:T(1,128)}, u32[]{:S(2)}) copy-start(s32[1,3]{1,0:T(1,128)} %param.7) | copy-start | bytes 40
  4.7 11.1 %copy-start.3 = (bf16[1,2,16384]{2,1,0:T(2,128)(2,1)S(1)}, bf16[1,2,16384]{2,1,0:T(2,128)(2,1)}, u32[]{:S(2)}) copy-start(bf16[1,2,16384]{2,1,0:T(2,128)(2,1)} %param.6) | copy-start | bytes 196612
  7.1 47.5 %all-to-all-start = ((bf16[8,2,16384]{2,1,0:T(2,128)(2,1)}), bf16[8,2,16384]{2,1,0:T(2,128)(2,1)S(1)}, u32[]{:S(2)}, u32[]{:S(2)}) async-start(bf16[8,2,16384]{2,1,0:T(2,128)(2,1)} %copy.65), calls=%async_computation | async-start | bytes 1048576 | tf_op jit(solution)/shard_map/all_to_all | solution.py:144
  16.0 8.8 %collective-permute-start.1 = (bf16[1,2,32768]{2,1,0:T(2,128)(2,1)S(1)}, bf16[1,2,32768]{2,1,0:T(2,128)(2,1)S(1)}, u32[]{:S(2)}, u32[]{:S(2)}) collective-permute-start(bf16[1,2,32768]{2,1,0:T(2,128)(2,1)S(1)} %broadcast_select_fusion.3), channel_id=1, source_target_pairs={{0,4},{2,6},{4,0},{6,2},{8,12},{10,14},{12,8},{14,10},{1,5},{3,7},... | collective-permute-start | bytes 393224 | tf_op jit(solution)/shard_map/ppermute | solution.py:16
  25.2 13.8 %collective-permute-start.2 = (bf16[1,2,65536]{2,1,0:T(2,128)(2,1)S(1)}, bf16[1,2,65536]{2,1,0:T(2,128)(2,1)S(1)}, u32[]{:S(2)}, u32[]{:S(2)}) collective-permute-start(bf16[1,2,65536]{2,1,0:T(2,128)(2,1)S(1)} %broadcast_select_fusion.1), channel_id=1, source_target_pairs={{0,8},{2,10},{4,12},{6,14},{8,0},{10,2},{12,4},{14,6},{1,9},{3,11}... | collective-permute-start | bytes 786440 | tf_op jit(solution)/shard_map/ppermute | solution.py:16
  65.1 1.5 %copy-start = (f32[1,32,4096]{2,1,0:T(8,128)S(1)}, f32[1,32,4096]{2,1,0:T(8,128)}, u32[]{:S(2)}) copy-start(f32[1,32,4096]{2,1,0:T(8,128)} %reshape.1495) | copy-start | bytes 1572868
  102.2 4.2 %copy-start.1 = (bf16[1,64,32,64]{1,2,0,3:T(8,128)(2,1)S(1)}, bf16[1,64,32,64]{1,2,0,3:T(8,128)(2,1)}, u32[]{:S(2)}) copy-start(bf16[1,64,32,64]{1,2,0,3:T(8,128)(2,1)} %get-tuple-element.31) | copy-start | bytes 786436
  108.6 1.3 %copy-start.2 = (f32[131072]{0:T(1024)S(1)}, f32[131072]{0:T(1024)}, u32[]{:S(2)}) copy-start(f32[131072]{0:T(1024)} %reshape.1590) | copy-start | bytes 1572868
